TPU v7x, 512 devices: a whole 4x4x16 slice. The times are simulated.
512 devices in a mesh: visit: 8 (over x, y_hi), patch: 64 (over z, y_lo, core).
Axes of the slice: x: 4, y: 4 (y_hi: 2, y_lo: 2; y = y_hi * 2 + y_lo), z: 16, core: 2. Of those that a mesh axis runs over, the one named last changes fastest.
Arguments:
- images: bfloat16 [8, 2048, 128, 128], P('visit', 'patch'), may hold values from -6 to 6
- intersection: int32 [8, 2048, 2], P('visit', 'patch'), may hold values from 0 to 63, all different within a row; in each aligned block of 32 rows (0 to 31, 32 to 63, ..., all dimensions but the last counted through in order) at most 2 rows name the same one
- offsets: int32 [8, 2048, 2, 2], P('visit', 'patch'), may hold values from 0 to 127
- subpixel: bfloat16 [8, 2048, 2, 2], P('visit', 'patch'), may hold values from 0 to 1
- variance: bfloat16 [8, 2048], P('visit', 'patch'), may hold values from 0.099609375 to 10
- basis_index: int32 [8, 2048], P('visit', 'patch'), may hold values from 0 to 63
- coefficients: float32 [64, 3, 3], replicated, may hold values from -4 to 4
Outputs:
- significance: float32 [64, 256, 256], P('patch', 'visit')
Inputs may be any that keep to these rules, and one draw needn't show every extreme that they name: `intersection`: each cell's 2 entries are different patches; among the 32 cells held by one device no patch is named more than 2 times, and in every draw some device's cells name some patch exactly 2 times.
All inputs are finite; a program needn't handle non-finite values.
Results may differ from a plain program's by a relative error of at most 0.0053.
Values may be sent and summed in bfloat16 or wider, within the bound.
A program may use at most 64 MiB of HBM per device.

v0:
```python
import math

import jax
import jax.numpy as jnp
from jax import lax
from jax.sharding import PartitionSpec as P

PPIX = 256
NB = 3


def kernel_tables(block_side):
    places = jnp.arange(block_side, dtype=jnp.float32)
    spread = places[:, None] - places[None, :]
    widths = 2.0 ** jnp.arange(NB, dtype=jnp.float32)
    profile = jnp.exp(-spread[None] ** 2 / (2.0 * widths[:, None, None] ** 2))
    return (profile / (math.sqrt(2.0 * math.pi) * widths[:, None, None])).astype(jnp.bfloat16)


def mixing_rows(set_ids, coefficients):
    set_total = coefficients.shape[0]
    chooser = (set_ids[:, None] == jnp.arange(set_total, dtype=jnp.int32)[None, :]).astype(
        jnp.float32
    )
    flat_table = coefficients.reshape(set_total, NB * 3)
    return jnp.dot(chooser, flat_table, precision=lax.Precision.HIGHEST).reshape(
        set_ids.shape[0], NB, 3
    )


def match_blocks(blocks_in, mixing, kernels):
    how_many = blocks_in.shape[0]
    block_side = blocks_in.shape[-1]
    stacked = jnp.transpose(kernels, (2, 0, 1)).reshape(block_side, NB * block_side)
    rows_done = jnp.einsum(
        "nia,ab->nib", blocks_in, stacked, preferred_element_type=jnp.float32
    ).astype(jnp.bfloat16)
    rows_done = rows_done.reshape(how_many, block_side, NB, block_side)
    smoothed = jnp.einsum("kia,nakj->nkij", kernels, rows_done, preferred_element_type=jnp.float32)
    ramp_axis = (2.0 * jnp.arange(block_side, dtype=jnp.float32) - (block_side - 1)) / (
        block_side - 1
    )
    mix_map = (
        mixing[:, :, 0, None, None]
        + mixing[:, :, 1, None, None] * ramp_axis[None, None, :, None]
        + mixing[:, :, 2, None, None] * ramp_axis[None, None, None, :]
    )
    return jnp.sum(mix_map * smoothed, axis=1).astype(jnp.bfloat16)


def placement(offset, fraction, out_rows, block_side):
    out_index = jnp.arange(out_rows, dtype=jnp.int32)[None, :, None]
    in_index = jnp.arange(block_side, dtype=jnp.int32)[None, None, :]
    distance = out_index - in_index - offset[:, None, None]
    share = fraction[:, None, None]
    return (
        jnp.where(distance == 0, 1.0 - share, 0.0) + jnp.where(distance == 1, share, 0.0)
    ).astype(jnp.bfloat16)


def body(images, intersection, offsets, subpixel, variance, basis_index, coefficients):
    block_count = images.shape[1]
    block_side = images.shape[2]
    top_count = intersection.shape[2]
    patch_count = lax.axis_size("patch")
    capacity = 2 * max(1, block_count * top_count // patch_count)
    slot_count = patch_count * capacity
    row_count = block_count * top_count
    kernels = kernel_tables(block_side)
    target = intersection[0].reshape(row_count)
    matches = (target[:, None] == jnp.arange(patch_count, dtype=jnp.int32)[None, :]).astype(
        jnp.int32
    )
    earlier = jnp.cumsum(matches, axis=0) - matches
    place_in = jnp.sum(earlier * matches, axis=1)
    slot_of = target * capacity + place_in
    chooser = (slot_of[None, :] == jnp.arange(slot_count, dtype=jnp.int32)[:, None]).astype(
        jnp.int32
    )
    filled = jnp.sum(chooser, axis=1)
    source_row = jnp.sum(chooser * jnp.arange(row_count, dtype=jnp.int32)[None, :], axis=1)
    source_block = source_row // top_count
    own_group = math.gcd(block_count, 16)
    own_mixing = mixing_rows(basis_index[0], coefficients)
    own_matched = lax.map(
        lambda grouped: match_blocks(grouped[0], grouped[1], kernels),
        (
            images[0].reshape(block_count // own_group, own_group, block_side, block_side),
            own_mixing.reshape(block_count // own_group, own_group, NB, 3),
        ),
    )
    own_matched = own_matched.reshape(block_count, block_side, block_side)
    shifts = offsets[0].reshape(row_count, 2)
    set_rows = jnp.repeat(basis_index[0], top_count)
    int_rows = jnp.stack([shifts[:, 0], shifts[:, 1], set_rows], axis=1)
    int_slots = jnp.concatenate([jnp.take(int_rows, source_row, axis=0), filled[:, None]], axis=1)
    float_rows = jnp.concatenate(
        [subpixel[0].reshape(row_count, 2), jnp.repeat(variance[0], top_count)[:, None]], axis=1
    )
    float_slots = jnp.take(float_rows, source_row, axis=0)
    float_slots = jnp.where(filled[:, None] > 0, float_slots, jnp.ones_like(float_slots))
    payload = jnp.take(own_matched, source_block, axis=0)
    got_blocks, got_ints, got_floats = (
        lax.all_to_all(
            payload.reshape(patch_count, capacity, block_side, block_side),
            "patch",
            split_axis=0,
            concat_axis=0,
            tiled=True,
        ),
        lax.all_to_all(
            int_slots.reshape(patch_count, capacity, 4),
            "patch",
            split_axis=0,
            concat_axis=0,
            tiled=True,
        ),
        lax.all_to_all(
            float_slots.reshape(patch_count, capacity, 3),
            "patch",
            split_axis=0,
            concat_axis=0,
            tiled=True,
        ),
    )
    group = math.gcd(slot_count, 16)
    group_turns = slot_count // group
    got_ints = got_ints.reshape(slot_count, 4)
    got_floats = got_floats.reshape(slot_count, 3).astype(jnp.float32)
    inverse_var = jnp.where(got_ints[:, 3] > 0, 1.0 / got_floats[:, 2], 0.0)
    packed = (
        got_blocks.reshape((group_turns, group) + got_blocks.shape[-2:]),
        got_ints.reshape(group_turns, group, 4),
        got_floats.reshape(group_turns, group, 3),
        inverse_var.reshape(group_turns, group),
    )

    def accumulate(totals, batch_in):
        numerator, weight = totals
        blocks_in, ints_in, floats_in, scale_in = batch_in
        down_place = placement(ints_in[:, 0], floats_in[:, 0], PPIX, block_side)
        across = placement(ints_in[:, 1], floats_in[:, 1], PPIX, block_side)
        placed = jnp.einsum("sij,skj->sik", blocks_in, across, preferred_element_type=jnp.float32)
        placed = (scale_in[:, None, None] * placed).astype(jnp.bfloat16)
        inner_width = group * block_side
        down_wide = jnp.transpose(down_place, (1, 0, 2)).reshape(PPIX, inner_width)
        numerator = numerator + jnp.dot(
            down_wide, placed.reshape(inner_width, PPIX), preferred_element_type=jnp.float32
        )
        down_sum = jnp.sum(down_place.astype(jnp.float32), axis=2)
        across_sum = jnp.sum(across.astype(jnp.float32), axis=2)
        weight = weight + jnp.dot(
            jnp.transpose(scale_in[:, None] * down_sum), across_sum, precision=lax.Precision.HIGHEST
        )
        return ((numerator, weight), None)

    start_totals = (jnp.zeros((PPIX, PPIX), jnp.float32), jnp.zeros((PPIX, PPIX), jnp.float32))
    (numerator, weight), _ = lax.scan(accumulate, start_totals, packed)
    numer_rows, weight_rows = (
        lax.psum_scatter(numerator[None], "visit", scatter_dimension=1, tiled=True),
        lax.psum_scatter(weight[None], "visit", scatter_dimension=1, tiled=True),
    )
    return numer_rows / jnp.sqrt(weight_rows + 1.0)


def solution(mesh):
    return jax.shard_map(
        body,
        mesh=mesh,
        in_specs=(
            P("visit", "patch", None, None),
            P("visit", "patch", None),
            P("visit", "patch", None, None),
            P("visit", "patch", None, None),
            P("visit", "patch"),
            P("visit", "patch"),
            P(),
        ),
        out_specs=P("patch", "visit", None),
        check_vma=False,
    )
```

profile of v0, /device:TPU:1, one launch (start us, length us, event | category | flops | bytes accessed | tf_op | source)
XLA Modules:
  0.0 491.5 jit_solution(10512958894656742895)
XLA Ops:
  11.7 18.2 %all-to-all-start.1 = ((bf16[64,2,3]{2,1,0:T(2,128)(2,1)}), bf16[64,2,3]{2,1,0:T(2,128)(2,1)S(1)}, u32[]{:S(2)}, u32[]{:S(2)}) async-start(bf16[64,2,3]{2,1,0:T(2,128)(2,1)} %broadcast_select_fusion.1), calls=%async_computation.1 | async-start | bytes 65536 | tf_op jit(solution)/shard_map/all_to_all | solution.py:118
  35.6 10.4 %while.27 = (s32[]{:T(128)}, bf16[2,16,128,128]{2,3,1,0:T(8,128)(2,1)}, f32[2,16,3,3]{1,2,3,0:T(4,128)S(1)}, bf16[2,16,128,128]{3,2,1,0:T(8,128)(2,1)}, f32[3]{0...) while((s32[]{:T(128)}, bf16[2,16,128,128]{2,3,1,0:T(8,128)(2,1)}, ...), condition=%wide.region_5.6_spmd.clone.clone, body=%wide.region_3.5_spmd.clone.clone.sunk | while | flops 405850496 | bytes 17207812 | solution.py:85
  35.8 1.6 convolution_convert_fusion.2
  38.4 1.3 fusion.65
  41.0 1.6 convolution_convert_fusion.2
  46.7 4.3 gather_fusion.2
  51.0 6.3 %copy.87 = bf16[128,128,128]{2,1,0:T(8,128)(2,1)} copy(bf16[128,128,128]{1,2,0:T(8,128)(2,1)} %gather_fusion.2) | data formatting | bytes 8388608 | tf_op jit(solution)/shard_map/jit(_take)/gather | solution.py:102
  57.3 13.6 %all-to-all-start = ((s32[64,2,4]{2,1,0:T(2,128)}), s32[64,2,4]{2,1,0:T(2,128)S(1)}, u32[]{:S(2)}, u32[]{:S(2)}) async-start(s32[64,2,4]{2,1,0:T(2,128)} %pad_add_fusion), calls=%async_computation | async-start | bytes 131072 | tf_op jit(solution)/shard_map/all_to_all | solution.py:111
  70.9 4.6 broadcast_select_fusion
  75.5 9.8 %all-to-all-done = s32[64,2,4]{2,1,0:T(2,128)S(1)} async-done(((s32[64,2,4]{2,1,0:T(2,128)}), s32[64,2,4]{2,1,0:T(2,128)S(1)}, u32[]{:S(2)}, u32[]{:S(2)}) %all-to-all-start) | async-done | bytes 2080 | tf_op jit(solution)/shard_map/all_to_all | solution.py:111
  85.3 5.4 %all-to-all-start.2 = ((bf16[64,2,128,128]{3,2,1,0:T(8,128)(2,1)}), bf16[64,2,128,128]{3,2,1,0:T(8,128)(2,1)}, u32[]{:S(2)}, u32[]{:S(2)}) async-start(bf16[64,2,128,128]{3,2,1,0:T(8,128)(2,1)} %broadcast_select_fusion), calls=%async_computation.2 | async-start | bytes 8388608 | tf_op jit(solution)/shard_map/all_to_all | solution.py:104
  91.7 184.8 %all-to-all-done.2 = bf16[64,2,128,128]{3,2,1,0:T(8,128)(2,1)} async-done(((bf16[64,2,128,128]{3,2,1,0:T(8,128)(2,1)}), bf16[64,2,128,128]{3,2,1,0:T(8,128)(2,1)}, u32[]{:S(2)}, u32[]{:S(2)}) %all-to-all-start.2) | async-done | bytes 4194336 | tf_op jit(solution)/shard_map/all_to_all | solution.py:104
  276.5 36.0 %while.28 = (s32[]{:T(128)}, f32[256,256]{1,0:T(8,128)S(1)}, f32[256,256]{1,0:T(8,128)S(1)}, s32[8,16,4]{1,2,0:T(4,128)S(1)}, f32[8,16,3]{1,0,2:T(8,128)S(1)}, /...) while((s32[]{:T(128)}, f32[256,256]{1,0:T(8,128)S(1)}, ...), condition=%wide.region_10.11_spmd.clone, body=%wide.region_7.10_spmd.clone.sunk | while | flops 433352736 | bytes 2169524 | solution.py:158
  276.6 1.4 convert_reduce_fusion.4
  278.6 2.4 fusion.70
  281.1 1.4 convert_reduce_fusion.4
  283.1 2.4 fusion.70
  285.6 1.4 convert_reduce_fusion.4
  287.6 2.4 fusion.70
  290.1 1.4 convert_reduce_fusion.4
  292.1 2.4 fusion.70
  294.6 1.4 convert_reduce_fusion.4
  296.6 2.4 fusion.70
  299.2 1.4 convert_reduce_fusion.4
  301.1 2.4 fusion.70
  303.7 1.4 convert_reduce_fusion.4
  305.6 2.4 fusion.70
  308.2 1.4 convert_reduce_fusion.4
  310.1 2.4 fusion.70
  314.0 79.6 %reduce-scatter.3.cloned.1.call-done = f32[1,32,256]{2,1,0:T(8,128)} async-done(((f32[1,256,256]{2,1,0:T(8,128)}), f32[1,32,256]{2,1,0:T(8,128)}) %reduce-scatter.3.cloned.1.call-update) | async-done | bytes 32784 | tf_op jit(solution)/shard_map/reduce_scatter | solution.py:160
  393.6 89.7 %reduce-scatter.5.cloned.1.call-done = f32[1,32,256]{2,1,0:T(8,128)} async-done(((f32[1,256,256]{2,1,0:T(8,128)}), f32[1,32,256]{2,1,0:T(8,128)}) %reduce-scatter.5.cloned.1.call-update) | async-done | bytes 32784 | tf_op jit(solution)/shard_map/reduce_scatter | solution.py:161
  483.3 1.4 rsqrt_multiply_fusion
  (156 shorter events, 24.7 us)
Async XLA Ops:
  11.7 45.7 %all-to-all-start.1 = ((bf16[64,2,3]{2,1,0:T(2,128)(2,1)}), bf16[64,2,3]{2,1,0:T(2,128)(2,1)S(1)}, u32[]{:S(2)}, u32[]{:S(2)}) async-start(bf16[64,2,3]{2,1,0:T(2,128)(2,1)} %broadcast_select_fusion.1), calls=%async_computation.1 | async-start | bytes 65536 | tf_op jit(solution)/shard_map/all_to_all | solution.py:118
  38.4 1.3 copy-start
  39.8 1.0 copy-start.1
  43.6 1.3 copy-start
  44.9 1.0 copy-start.1
  57.3 28.0 %all-to-all-start = ((s32[64,2,4]{2,1,0:T(2,128)}), s32[64,2,4]{2,1,0:T(2,128)S(1)}, u32[]{:S(2)}, u32[]{:S(2)}) async-start(s32[64,2,4]{2,1,0:T(2,128)} %pad_add_fusion), calls=%async_computation | async-start | bytes 131072 | tf_op jit(solution)/shard_map/all_to_all | solution.py:111
  85.3 191.2 %all-to-all-start.2 = ((bf16[64,2,128,128]{3,2,1,0:T(8,128)(2,1)}), bf16[64,2,128,128]{3,2,1,0:T(8,128)(2,1)}, u32[]{:S(2)}, u32[]{:S(2)}) async-start(bf16[64,2,128,128]{3,2,1,0:T(8,128)(2,1)} %broadcast_select_fusion), calls=%async_computation.2 | async-start | bytes 8388608 | tf_op jit(solution)/shard_map/all_to_all | solution.py:104
  90.8 302.9 %reduce-scatter.3.cloned.1.call-start = ((), (), s32[]{:S(2)}) async-start(), calls=%async_computation.5 | async-start | bytes 294912 | tf_op jit(solution)/shard_map/reduce_scatter | solution.py:160
  312.6 0.7 copy-start.3
  312.6 0.8 copy-start.2
  313.3 170.0 %reduce-scatter.5.cloned.1.call-start = ((), (), s32[]{:S(2)}) async-start(), calls=%async_computation.6 | async-start | bytes 294912 | tf_op jit(solution)/shard_map/reduce_scatter | solution.py:161
Sparse Core Ops, SparseCore 0:
  313.4 80.1 reduce-scatter.2
  398.7 84.5 reduce-scatter.4
where the time goes:
time: 493 us; the launch traced here: 492 us
  waiting for transfers between devices  365 us (74%)
  starting transfers between devices  37.2 us (8%)
  matrix products  30 us (6%)
  local copies, waits for them, and re-layouts  24.3 us (5%)
  other arithmetic  20.9 us (4%)
  between operations  13.6 us (3%)
    all_to_all x1, waiting for transfers between devices, body(): lax.all_to_all(payload.reshape(patch_count, capacity, block_side, block_s...  185 us
    reduce_scatter x1, waiting for transfers between devices, body(): lax.psum_scatter(weight[None], 'visit', scatter_dimension=1, tiled=True)  89.7 us
    reduce_scatter x1, waiting for transfers between devices, body(): lax.psum_scatter(numerator[None], 'visit', scatter_dimension=1, tiled=True)  79.6 us
    dot_general x8, matrix products, accumulate(): jnp.dot(down_wide, placed.reshape(inner_width, PPIX), preferred_element_t...  19.4 us
    all_to_all x1, starting transfers between devices, body(): lax.all_to_all(float_slots.reshape(patch_count, capacity, 3), 'patch', sp...  18.2 us
    all_to_all x1, starting transfers between devices, body(): lax.all_to_all(int_slots.reshape(patch_count, capacity, 4), 'patch', spli...  13.6 us
    reduce_sum x8, other arithmetic, accumulate(): down_sum = jnp.sum(down_place.astype(jnp.float32), axis=2)  10.8 us
    gather x2, local copies, waits for them, and re-layouts, body(): payload = jnp.take(own_matched, source_block, axis=0)  10.6 us
  transfers between devices with their start and end apart: 5, of which 4 were waited for; matrix products, arithmetic and copies ran while one was open for 6% of the time, Pallas kernels for 0%

commit v1 on v0

v1 whole, which is shorter than its diff:
```python
import math

import jax
import jax.numpy as jnp
from jax import lax
from jax.experimental import pallas as pl
from jax.experimental.pallas import tpu as pltpu
from jax.sharding import PartitionSpec as P

PIX = 128
PPIX = 256
NB = 3
CELLS = 32
PAIRS = 64
PATCHES = 64
DEPTH = 16
PARTS = 4
ROWS = 32
F32, BF16, I32 = jnp.float32, jnp.bfloat16, jnp.int32
MESH = pl.DeviceIdType.MESH
VMEM_LIMIT = 56 * 1024 * 1024


def distance_at(k):
    if isinstance(k, int):
        return 8 + k // 2 if k % 2 == 0 else 7 - k // 2
    return jnp.where(k % 2 == 0, 8 + k // 2, 7 - k // 2)


def position():
    v, p = lax.axis_index("visit"), lax.axis_index("patch")
    return v // 2, (v % 2) * 2 + (p // 2) % 2, p // 4, p % 2


def device_at(x, y, z, c):
    return {"visit": x * 2 + y // 2, "patch": z * 4 + (y % 2) * 2 + c}


def iota(shape, axis):
    return lax.broadcasted_iota(I32, shape, axis)


def local_kernel(
    inter, offs, frac, inv, basis, coef, images, target_row, target_col, fields,
    tiles, meta, matched, table, count,
):
    x, y, z, c = position()

    @pl.loop(0, PATCHES)
    def _(i):
        count[i] = 0
        table[2 * i] = -1
        table[2 * i + 1] = -1

    @pl.loop(0, PAIRS)
    def _(s):
        p = inter[s]
        rank = count[p]
        table[2 * p + rank] = s
        count[p] = rank + 1

    spread = (iota((PIX, PIX), 0) - iota((PIX, PIX), 1)).astype(F32)
    kernels = []
    for k in range(NB):
        width = 2.0**k
        profile = jnp.exp(-(spread**2) / (2.0 * width**2))
        kernels.append((profile / (math.sqrt(2.0 * math.pi) * width)).astype(BF16))
    stacked = jnp.concatenate(kernels, axis=1)
    ramp_i = (2.0 * iota((PIX, PIX), 0).astype(F32) - (PIX - 1)) / (PIX - 1)
    ramp_j = (2.0 * iota((PIX, PIX), 1).astype(F32) - (PIX - 1)) / (PIX - 1)

    @pl.loop(0, CELLS // 2)
    def _(g):
        rows = jnp.dot(
            images[pl.ds(2 * g, 2)].reshape(2 * PIX, PIX), stacked, preferred_element_type=F32
        ).astype(BF16)
        total = [None, None]
        for k in range(NB):
            part = rows[:, k * PIX : (k + 1) * PIX]
            wide = jnp.concatenate([part[:PIX], part[PIX:]], axis=1)
            smooth = jnp.dot(kernels[k], wide, preferred_element_type=F32)
            for b in range(2):
                at = basis[2 * g + b] * (NB * 3) + 3 * k
                mix = coef[at] + coef[at + 1] * ramp_i + coef[at + 2] * ramp_j
                term = mix * smooth[:, b * PIX : (b + 1) * PIX]
                total[b] = term if k == 0 else total[b] + term
        for b in range(2):
            matched[2 * g + b] = total[b].astype(BF16)

    across_at = iota((PIX, PPIX), 1) - iota((PIX, PPIX), 0)
    down_at = iota((PPIX, PIX), 0) - iota((PPIX, PIX), 1)

    def one_hot(at, offset, share):
        return jnp.where(
            at == offset, 1.0 - share, jnp.where(at == offset + 1, share, 0.0)
        ).astype(BF16)

    @pl.loop(0, DEPTH)
    def _(k):
        z_to = lax.rem(z + distance_at(k), DEPTH)
        for r in range(2):
            for y_lo in range(2):
                p = z_to * 4 + y_lo * 2 + (c if r == 0 else 1 - c)
                downs, placed = [], []
                for slot in range(2):
                    s = table[2 * p + slot]
                    filled = s >= 0
                    s = jnp.maximum(s, 0)
                    scale = jnp.where(filled, inv[s // 2], 0.0)
                    across = one_hot(across_at, offs[2 * s + 1], frac[2 * s + 1])
                    wide = jnp.dot(matched[s // 2], across, preferred_element_type=F32)
                    placed.append((scale * wide).astype(BF16))
                    downs.append(one_hot(down_at, offs[2 * s], frac[2 * s]))
                tile = jnp.dot(
                    jnp.concatenate(downs, axis=1),
                    jnp.concatenate(placed, axis=0),
                    preferred_element_type=F32,
                ).astype(BF16)
                for x_to in range(4):
                    for y_hi in range(2):
                        at = (x_to * 2 + y_hi) * ROWS
                        y_to = y_hi * 2 + y_lo
                        block = tile[at : at + ROWS]
                        tiles[r, k // 4, 0, x_to, k % 4, y_to] = block[:, :PIX]
                        tiles[r, k // 4, 1, y_to, k % 4, x_to] = block[:, PIX:]

    same = target_col[...] == target_row[...]
    earlier = iota((PAIRS, PAIRS), 1) < iota((PAIRS, PAIRS), 0)
    rank = jnp.sum(jnp.where(same & earlier, 1, 0), axis=1, keepdims=True)
    code = 2 * target_col[...] + rank
    lane = iota((PAIRS, PIX), 1)
    mine = lane // 8 == z
    for k in range(DEPTH):
        z_to = lax.rem(z + distance_at(k), DEPTH)
        pick = jnp.where((code == z_to * 8 + lane % 8) & mine, 1.0, 0.0).astype(BF16)
        meta[k] = jnp.dot(fields[...], pick, preferred_element_type=F32)


class Copies:
    def __init__(self, send, recv):
        self.send, self.recv, self.used = send, recv, 0

    def new(self, src, dst, device):
        at = self.used
        self.used += 1
        return pltpu.make_async_remote_copy(
            src_ref=src,
            dst_ref=dst,
            send_sem=self.send.at[at],
            recv_sem=self.recv.at[at],
            device_id=device,
            device_id_type=MESH,
        )


def add_into(dst, src):
    dst[...] = (dst[...].astype(F32) + src[...].astype(F32)).astype(BF16)


class Ring:
    def __init__(self, copies, me, device, blocks, relay, fin):
        half = blocks.shape[1] // 2
        lo, hi = pl.ds(0, half), pl.ds(half, half)
        right, left, far = (me + 1) % 4, (me + 3) % 4, (me + 2) % 4
        to_right, to_left = device(right), device(left)
        self.blocks, self.relay, self.fin = blocks, relay, fin
        self.me, self.left, self.right, self.lo, self.hi = me, left, right, lo, hi
        self.first = [
            copies.new(blocks.at[far, lo], relay.at[0], to_right),
            copies.new(blocks.at[far, hi], relay.at[1], to_left),
            copies.new(blocks.at[right, hi], fin.at[0, hi], to_right),
            copies.new(blocks.at[left, lo], fin.at[1, lo], to_left),
        ]
        self.second = [
            copies.new(blocks.at[right, lo], fin.at[0, lo], to_right),
            copies.new(blocks.at[left, hi], fin.at[1, hi], to_left),
        ]

    def start(self):
        for copy in self.first:
            copy.start()

    def forward(self):
        self.first[0].wait_recv()
        add_into(self.blocks.at[self.right, self.lo], self.relay.at[0])
        self.second[0].start()
        self.first[1].wait_recv()
        add_into(self.blocks.at[self.left, self.hi], self.relay.at[1])
        self.second[1].start()

    def finish(self):
        for copy in self.first[2:] + self.second:
            copy.wait_recv()

    def result(self, i):
        own = self.blocks[self.me, i].astype(F32)
        return own + self.fin[0, i].astype(F32) + self.fin[1, i].astype(F32)

    def drain(self):
        for copy in self.first + self.second:
            copy.wait_send()


def share_kernel(
    tiles, meta, out,
    core_in, relay1, fin1, blocks2, relay2, fin2, blocks3, far_in,
    meta_z, meta_x, meta_y, meta_c, send_sem, recv_sem,
):
    x, y, z, c = position()
    peers = [device_at(x, y, z, 1 - c)]
    peers += [device_at((x + d) % 4, y, z, c) for d in (1, 2, 3)]
    peers += [device_at(x, (y + d) % 4, z, c) for d in (1, 2, 3)]
    peers += [device_at(x, y, (z + d) % DEPTH, c) for d in range(1, DEPTH)]
    barrier = pltpu.get_barrier_semaphore()
    for peer in peers:
        pl.semaphore_signal(barrier, inc=1, device_id=peer, device_id_type=MESH)
    pl.semaphore_wait(barrier, len(peers))

    copies = Copies(send_sem, recv_sem)
    x_device = lambda to: device_at(to, y, z, c)
    y_device = lambda to: device_at(x, to, z, c)
    z_device = lambda k: device_at(x, y, (z + distance_at(k)) % DEPTH, c)

    core = [
        copies.new(tiles.at[1, q], core_in.at[q], device_at(x, y, z, 1 - c)) for q in range(PARTS)
    ]
    for copy in core:
        copy.start()

    meta_copies = [copies.new(meta.at[k], meta_z.at[k], z_device(k)) for k in range(DEPTH - 1)]
    for copy in meta_copies:
        copy.start()
    meta_z[DEPTH - 1] = meta[DEPTH - 1]

    rings1, rings2, sent3 = {}, {}, []

    def enter(q):
        core[q].wait_recv()

        for half in range(2):
            @pl.loop(0, 4)
            def _(i, half=half):
                add_into(core_in.at[q, half, i], tiles.at[0, q, half, i])

        for half in range(2):
            me, device = ((x, x_device), (y, y_device))[half]
            rings1[q, half] = Ring(
                copies, me, device, core_in.at[q, half], relay1.at[q, half], fin1.at[q, half]
            )
            rings1[q, half].start()

    def middle(q):
        for half in range(2):
            rings1[q, half].forward()

    def turn(q):
        for half in range(2):
            ring = rings1[q, half]
            ring.finish()
            for i in range(4):
                block = ring.result(i).astype(BF16)
                for other in range(4):
                    blocks2[q, half, other, i] = block[other]
            me, device = ((y, y_device), (x, x_device))[half]
            rings2[q, half] = Ring(
                copies, me, device, blocks2.at[q, half], relay2.at[q, half], fin2.at[q, half]
            )
            rings2[q, half].start()

    def middle2(q):
        for half in range(2):
            rings2[q, half].forward()

    def leave(q):
        for half in range(2):
            ring = rings2[q, half]
            ring.finish()
            for i in range(4):
                k = 4 * q + i
                if k < DEPTH - 1:
                    blocks3[k, half] = ring.result(i).astype(BF16)
                else:
                    far_in[k, half] = ring.result(i).astype(BF16)
        for i in range(4):
            k = 4 * q + i
            if k < DEPTH - 1:
                copy = copies.new(blocks3.at[k], far_in.at[k], z_device(k))
                copy.start()
                sent3.append(copy)

    def meta_plane():
        for copy in meta_copies:
            copy.wait_recv()
        total = meta_z[0]
        for k in range(1, DEPTH):
            total = total + meta_z[k]
        meta_x[x] = total
        sent = []
        for d in (1, 2, 3):
            sent.append(copies.new(meta_x.at[x], meta_x.at[x], x_device((x + d) % 4)))
        for copy in sent:
            copy.start()
        meta_copies.extend(sent)
        return sent

    def meta_second(before):
        for copy in before:
            copy.wait_recv()
        meta_y[y] = meta_x[...]
        sent = []
        for d in (1, 2, 3):
            sent.append(copies.new(meta_y.at[y], meta_y.at[y], y_device((y + d) % 4)))
        for copy in sent:
            copy.start()
        meta_copies.extend(sent)
        return sent

    def meta_third(before):
        for copy in before:
            copy.wait_recv()
        copy = copies.new(meta_y, meta_c, device_at(x, y, z, 1 - c))
        copy.start()
        meta_copies.append(copy)
        return copy

    enter(0)
    enter(1)
    middle(0)
    sent_x = meta_plane()
    enter(2)
    turn(0)
    middle(1)
    sent_y = meta_second(sent_x)
    enter(3)
    middle2(0)
    turn(1)
    middle(2)
    sent_c = meta_third(sent_y)
    leave(0)
    middle2(1)
    turn(2)
    middle(3)
    leave(1)
    middle2(2)
    turn(3)
    leave(2)
    middle2(3)

    sent_c.wait_recv()
    combo = (y % 2) * 2 + c
    lane = iota((8, PIX), 1)
    mine = (lane // 2) % 4 == combo
    row_at = (iota((ROWS, PIX), 0) + (x * 2 + y // 2) * ROWS).astype(F32)
    column_at = iota((PPIX, PIX), 0).astype(F32)

    def cover(at, offset, share):
        rest = (1.0 - share).astype(BF16).astype(F32)
        d = at - offset
        first = jnp.where((d >= 0.0) & (d < float(PIX)), rest, 0.0)
        return first + jnp.where((d >= 1.0) & (d < float(PIX + 1)), share, 0.0)

    weight = jnp.zeros((ROWS, PPIX), F32)
    for source in (meta_y, meta_c):
        for b in range(4):
            full = jnp.zeros((8, PIX), F32)
            for m in range(4):
                kept = jnp.where(mine, source[b, m], 0.0)
                full = full + pltpu.roll(kept, (2 * (m - combo)) % PIX, 1)
            valid = full[5:6] > 0.0
            inverse = jnp.where(valid, 1.0 / jnp.where(valid, full[4:5], 1.0), 0.0)
            down = inverse * cover(row_at, full[0:1], full[2:3])
            across = cover(column_at, full[1:2], full[3:4])
            weight = weight + lax.dot_general(
                down, across, (((1,), (1,)), ((), ())),
                precision=lax.Precision.HIGHEST, preferred_element_type=F32,
            )

    leave(3)
    for copy in sent3:
        copy.wait_recv()
    for half in range(2):
        total = far_in[0, half].astype(F32)
        for k in range(1, DEPTH):
            total = total + far_in[k, half].astype(F32)
        across = slice(half * PIX, (half + 1) * PIX)
        out[:, across] = total / jnp.sqrt(weight[:, across] + 1.0)

    for copy in core + meta_copies + sent3:
        copy.wait_send()
    for ring in list(rings1.values()) + list(rings2.values()):
        ring.drain()


COPY_COUNT = PARTS + PARTS * 24 + (DEPTH - 1) * 2 + 7


def body(images, intersection, offsets, subpixel, variance, basis_index, coefficients):
    target = intersection[0].reshape(PAIRS)
    shifts = offsets[0].reshape(PAIRS, 2)
    shares = subpixel[0].reshape(PAIRS, 2).astype(F32)
    inverse = 1.0 / variance[0].astype(F32)
    spare = jnp.zeros((PAIRS,), BF16)
    fields = jnp.stack(
        [
            shifts[:, 0].astype(BF16),
            shifts[:, 1].astype(BF16),
            subpixel[0].reshape(PAIRS, 2)[:, 0],
            subpixel[0].reshape(PAIRS, 2)[:, 1],
            jnp.repeat(variance[0], 2),
            spare + 1,
            spare,
            spare,
        ]
    )
    smem = pl.BlockSpec(memory_space=pltpu.SMEM)
    vmem = pl.BlockSpec(memory_space=pltpu.VMEM)
    tiles, meta = pl.pallas_call(
        local_kernel,
        out_shape=(
            jax.ShapeDtypeStruct((2, PARTS, 2, 4, 4, 4, ROWS, PIX), BF16),
            jax.ShapeDtypeStruct((DEPTH, 8, PIX), F32),
        ),
        in_specs=[smem] * 6 + [vmem] * 4,
        out_specs=(vmem, vmem),
        scratch_shapes=[
            pltpu.VMEM((CELLS, PIX, PIX), BF16),
            pltpu.SMEM((2 * PATCHES,), I32),
            pltpu.SMEM((PATCHES,), I32),
        ],
        compiler_params=pltpu.CompilerParams(vmem_limit_bytes=VMEM_LIMIT),
    )(
        target,
        shifts.reshape(2 * PAIRS),
        shares.reshape(2 * PAIRS),
        inverse,
        basis_index[0],
        coefficients.reshape(-1),
        images[0],
        target.reshape(1, PAIRS),
        target.reshape(PAIRS, 1),
        fields,
    )
    out = pl.pallas_call(
        share_kernel,
        out_shape=jax.ShapeDtypeStruct((ROWS, PPIX), F32),
        in_specs=[vmem] * 2,
        out_specs=vmem,
        scratch_shapes=[
            pltpu.VMEM((PARTS, 2, 4, 4, 4, ROWS, PIX), BF16),
            pltpu.VMEM((PARTS, 2, 2, 2, 4, ROWS, PIX), BF16),
            pltpu.VMEM((PARTS, 2, 2, 4, 4, ROWS, PIX), BF16),
            pltpu.VMEM((PARTS, 2, 4, 4, ROWS, PIX), BF16),
            pltpu.VMEM((PARTS, 2, 2, 2, ROWS, PIX), BF16),
            pltpu.VMEM((PARTS, 2, 2, 4, ROWS, PIX), BF16),
            pltpu.VMEM((DEPTH - 1, 2, ROWS, PIX), BF16),
            pltpu.VMEM((DEPTH, 2, ROWS, PIX), BF16),
            pltpu.VMEM((DEPTH, 8, PIX), F32),
            pltpu.VMEM((4, 8, PIX), F32),
            pltpu.VMEM((4, 4, 8, PIX), F32),
            pltpu.VMEM((4, 4, 8, PIX), F32),
            pltpu.SemaphoreType.DMA((COPY_COUNT,)),
            pltpu.SemaphoreType.DMA((COPY_COUNT,)),
        ],
        compiler_params=pltpu.CompilerParams(
            collective_id=0, has_side_effects=True, vmem_limit_bytes=VMEM_LIMIT
        ),
    )(tiles, meta)
    return out[None]


def solution(mesh):
    return jax.shard_map(
        body,
        mesh=mesh,
        in_specs=(
            P("visit", "patch", None, None),
            P("visit", "patch", None),
            P("visit", "patch", None, None),
            P("visit", "patch", None, None),
            P("visit", "patch"),
            P("visit", "patch"),
            P(),
        ),
        out_specs=P("patch", "visit", None),
        check_vma=False,
    )
```

time: 493 us -> 98.9 us (0.20)
  waiting for transfers between devices: 365 us -> 0 us
  Pallas kernels: 0 us -> 84.6 us
  starting transfers between devices: 37.2 us -> 0 us
  matrix products: 30 us -> 0 us
  other arithmetic: 20.9 us -> 1.91 us
  between operations: 13.6 us -> 0.05 us
  local copies, waits for them, and re-layouts: 24.3 us -> 11.3 us
    all_to_all x3 -> x0, waiting for transfers between devices: 195 us -> none  [the longest x1 185 us: body(): lax.all_to_all(payload.reshape(patch_count, capacity, block_side, block_s...]
    reduce_scatter x2 -> x0, waiting for transfers between devices: 169 us -> none  [the longest x1 89.7 us: body(): lax.psum_scatter(weight[None], 'visit', scatter_dimension=1, tiled=True)]
    pallas_call x0 -> x2, Pallas kernels: none -> 84.6 us  [the longest x1 59.9 us: body(): pl.pallas_call(share_kernel, out_shape=jax.ShapeDtypeStruct((ROWS, PPIX),...]
    all_to_all x3 -> x0, starting transfers between devices: 37.1 us -> none  [the longest x1 18.2 us: body(): lax.all_to_all(float_slots.reshape(patch_count, capacity, 3), 'patch', sp...]
    dot_general x21 -> x0, matrix products: 30 us -> none  [the longest x8 19.4 us: accumulate(): jnp.dot(down_wide, placed.reshape(inner_width, PPIX), preferred_element_t...]
    gather x4 -> x0, local copies, waits for them, and re-layouts: 12 us -> none  [the longest x2 10.6 us: body(): payload = jnp.take(own_matched, source_block, axis=0)]
    reduce_sum x10 -> x0, other arithmetic: 11.1 us -> none  [the longest x8 10.8 us: accumulate(): down_sum = jnp.sum(down_place.astype(jnp.float32), axis=2)]
    select_n x5 -> x0, other arithmetic: 5.61 us -> none  [the longest x2 4.62 us: body(): payload = jnp.take(own_matched, source_block, axis=0)]
  transfers between devices with their start and end apart: 5 -> 0, of which waited for: 4 -> 0; matrix products, arithmetic and copies ran while one was open for 6% -> 0% of each run, Pallas kernels for 0% -> 0%
where the time goes in v1:
time: 98.9 us; the launch traced here: 97.9 us
  Pallas kernels  84.6 us (86%)
  local copies, waits for them, and re-layouts  11.3 us (11%)
  other arithmetic  1.91 us (2%)
    pallas_call x1, Pallas kernels, body(): pl.pallas_call(share_kernel, out_shape=jax.ShapeDtypeStruct((ROWS, PPIX),...  59.9 us
    pallas_call x1, Pallas kernels, body(): pl.pallas_call(local_kernel, out_shape=(jax.ShapeDtypeStruct((2, PARTS, 2...  24.7 us
    unnamed x5, local copies, waits for them, and re-layouts  4.51 us

profile of v1, /device:TPU:1, one launch (start us, length us, event | category | flops | bytes accessed | tf_op | source)
XLA Modules:
  0.0 97.9 jit_solution(12451910045431770030)
XLA Ops:
  0.0 1.2 %convert_divide_fusion.inv = f32[32]{0:T(128)} fusion(bf16[1,32]{1,0:T(2,128)(2,1)} %param.11), kind=kLoop, calls=%fused_computation.4 | loop fusion | flops 64 | bytes 192 | tf_op jit(solution)/shard_map/div | solution.py:401
  1.2 0.7 convert.6
  1.9 0.7 broadcast_in_dim.6
  2.6 0.1 stack_reshape.3
  2.8 0.1 copy.22
  2.9 0.1 reshape.31
  3.0 0.8 copy.16
  3.7 0.6 reshape_reshape_squeeze.10.target_row
  4.4 0.7 reshape_squeeze.11.inter
  5.0 0.7 reshape_reshape_squeeze.12.target_col
  5.7 0.8 copy.23
  6.5 0.1 reshape_squeeze.13
  6.7 0.6 stack.13.fields
  7.3 0.8 copy.17
  8.1 0.7 reshape_reshape_squeeze.9.offs
  8.8 0.8 copy.18
  9.5 0.7 reshape.30.frac
  10.3 0.8 copy.19
  11.1 0.8 reshape.29.coef
  11.9 24.7 %shard_map.73 = (bf16[2,4,2,4,4,4,32,128]{7,6,5,4,3,2,1,0:T(8,128)(2,1)}, f32[16,8,128]{2,1,0:T(8,128)}) custom-call(s32[64]{0:T(128)} %reshape_squeeze.11.inter, s32[128]{0:T(128)} %reshape_reshape_squeeze.9.offs, f32[128]{0:T(128)} %reshape.30.frac, f32[32]{0:T(128)} %convert_divide_fusion.inv, s32[32]{0:T(128)} %bitcast.23, f32[576]{0:T(1024)} %reshape.29.coef, ...), custom_call_target="tpu_custom_call" | custom-call | tf_op jit(solution)/shard_map/pallas_call | solution.py:417
  36.6 59.9 %shard_map.74 = f32[32,256]{1,0:T(8,128)} custom-call(bf16[2,4,2,4,4,4,32,128]{7,6,5,4,3,2,1,0:T(8,128)(2,1)} %get-tuple-element.7.tiles, f32[16,8,128]{2,1,0:T(8,128)} %get-tuple-element.8.meta), custom_call_target="tpu_custom_call" | custom-call | tf_op jit(solution)/shard_map/pallas_call | solution.py:443
  96.5 1.4 %copy.26 = f32[1,32,256]{2,1,0:T(8,128)} copy(f32[1,32,256]{2,1,0:T(8,128)} %bitcast.22) | data formatting | bytes 65536
  (3 shorter events, 0.0 us)

commit v2 on v1

--- a/solution.py
+++ b/solution.py
@@ -18,6 +18,7 @@
 ROWS = 32
 F32, BF16, I32 = jnp.float32, jnp.bfloat16, jnp.int32
 MESH = pl.DeviceIdType.MESH
+GROUP = 8
 VMEM_LIMIT = 56 * 1024 * 1024
 
 
@@ -40,24 +41,23 @@
     return lax.broadcasted_iota(I32, shape, axis)
 
 
-def local_kernel(
-    inter, offs, frac, inv, basis, coef, images, target_row, target_col, fields,
-    tiles, meta, matched, table, count,
+def match_kernel(
+    inter, offs, basis, coef, images, inter_v, offs_v, frac_v, var_v,
+    matched, table, shares, meta, shares_v, count, sem,
 ):
-    x, y, z, c = position()
-
-    @pl.loop(0, PATCHES)
+    z = position()[2]
+    for t in range(2):
+        for axis in range(2):
+            shares_v[2 * t + axis : 2 * t + axis + 1, :CELLS] = frac_v[t, axis : axis + 1].astype(F32)
+    shares_v[4:5, :CELLS] = 1.0 / var_v[...].astype(F32)
+    move = pltpu.make_async_copy(shares_v, shares, sem)
+    move.start()
+
+    @pl.loop(0, PATCHES, unroll=8)
     def _(i):
         count[i] = 0
         table[2 * i] = -1
         table[2 * i + 1] = -1
-
-    @pl.loop(0, PAIRS)
-    def _(s):
-        p = inter[s]
-        rank = count[p]
-        table[2 * p + rank] = s
-        count[p] = rank + 1
 
     spread = (iota((PIX, PIX), 0) - iota((PIX, PIX), 1)).astype(F32)
     kernels = []
@@ -69,71 +69,64 @@
     ramp_i = (2.0 * iota((PIX, PIX), 0).astype(F32) - (PIX - 1)) / (PIX - 1)
     ramp_j = (2.0 * iota((PIX, PIX), 1).astype(F32) - (PIX - 1)) / (PIX - 1)
 
-    @pl.loop(0, CELLS // 2)
+    @pl.loop(0, CELLS // GROUP)
     def _(g):
+        for b in range(GROUP):
+            for t in range(2):
+                p = inter[t, GROUP * g + b]
+                rank = count[p]
+                table[2 * p + rank] = 2 * (GROUP * g + b) + t
+                count[p] = rank + 1
         rows = jnp.dot(
-            images[pl.ds(2 * g, 2)].reshape(2 * PIX, PIX), stacked, preferred_element_type=F32
+            images[pl.ds(GROUP * g, GROUP)].reshape(GROUP * PIX, PIX),
+            stacked,
+            preferred_element_type=F32,
         ).astype(BF16)
-        total = [None, None]
+        total = [None] * GROUP
         for k in range(NB):
             part = rows[:, k * PIX : (k + 1) * PIX]
-            wide = jnp.concatenate([part[:PIX], part[PIX:]], axis=1)
+            wide = jnp.concatenate([part[b * PIX : (b + 1) * PIX] for b in range(GROUP)], axis=1)
             smooth = jnp.dot(kernels[k], wide, preferred_element_type=F32)
-            for b in range(2):
-                at = basis[2 * g + b] * (NB * 3) + 3 * k
-                mix = coef[at] + coef[at + 1] * ramp_i + coef[at + 2] * ramp_j
+            for b in range(GROUP):
+                q = basis[0, GROUP * g + b]
+                mix = coef[k, 0, q] + coef[k, 1, q] * ramp_i + coef[k, 2, q] * ramp_j
                 term = mix * smooth[:, b * PIX : (b + 1) * PIX]
                 total[b] = term if k == 0 else total[b] + term
-        for b in range(2):
-            matched[2 * g + b] = total[b].astype(BF16)
-
-    across_at = iota((PIX, PPIX), 1) - iota((PIX, PPIX), 0)
-    down_at = iota((PPIX, PIX), 0) - iota((PPIX, PIX), 1)
-
-    def one_hot(at, offset, share):
-        return jnp.where(
-            at == offset, 1.0 - share, jnp.where(at == offset + 1, share, 0.0)
-        ).astype(BF16)
-
-    @pl.loop(0, DEPTH)
-    def _(k):
-        z_to = lax.rem(z + distance_at(k), DEPTH)
-        for r in range(2):
-            for y_lo in range(2):
-                p = z_to * 4 + y_lo * 2 + (c if r == 0 else 1 - c)
-                downs, placed = [], []
-                for slot in range(2):
-                    s = table[2 * p + slot]
-                    filled = s >= 0
-                    s = jnp.maximum(s, 0)
-                    scale = jnp.where(filled, inv[s // 2], 0.0)
-                    across = one_hot(across_at, offs[2 * s + 1], frac[2 * s + 1])
-                    wide = jnp.dot(matched[s // 2], across, preferred_element_type=F32)
-                    placed.append((scale * wide).astype(BF16))
-                    downs.append(one_hot(down_at, offs[2 * s], frac[2 * s]))
-                tile = jnp.dot(
-                    jnp.concatenate(downs, axis=1),
-                    jnp.concatenate(placed, axis=0),
-                    preferred_element_type=F32,
-                ).astype(BF16)
-                for x_to in range(4):
-                    for y_hi in range(2):
-                        at = (x_to * 2 + y_hi) * ROWS
-                        y_to = y_hi * 2 + y_lo
-                        block = tile[at : at + ROWS]
-                        tiles[r, k // 4, 0, x_to, k % 4, y_to] = block[:, :PIX]
-                        tiles[r, k // 4, 1, y_to, k % 4, x_to] = block[:, PIX:]
-
-    same = target_col[...] == target_row[...]
-    earlier = iota((PAIRS, PAIRS), 1) < iota((PAIRS, PAIRS), 0)
-    rank = jnp.sum(jnp.where(same & earlier, 1, 0), axis=1, keepdims=True)
-    code = 2 * target_col[...] + rank
-    lane = iota((PAIRS, PIX), 1)
+        for b in range(GROUP):
+            matched[GROUP * g + b] = total[b].astype(BF16)
+
+    target = inter_v[...].astype(F32)
+    eye = (iota((CELLS, CELLS), 0) == iota((CELLS, CELLS), 1)).astype(F32).astype(BF16)
+    column = lax.dot_general(
+        eye, target.astype(BF16), (((1,), (1,)), ((), ())), preferred_element_type=F32
+    )
+    earlier = iota((CELLS, CELLS), 1) < iota((CELLS, CELLS), 0)
+    lane = iota((CELLS, PIX), 1)
     mine = lane // 8 == z
+    place = (lane % 8).astype(F32)
+    codes, fields = [], []
+    for t in range(2):
+        rank = jnp.zeros((CELLS, 1), F32)
+        for other in range(2):
+            same = (column[:, t : t + 1] == target[other : other + 1]) & earlier
+            rank = rank + jnp.sum(jnp.where(same, 1.0, 0.0), axis=1, keepdims=True)
+        codes.append(2.0 * column[:, t : t + 1] + rank)
+        row = iota((8, CELLS), 0)
+        field = jnp.where(row == 0, offs_v[t, 0:1].astype(F32), 0.0)
+        field = jnp.where(row == 1, offs_v[t, 1:2].astype(F32), field)
+        field = jnp.where(row == 2, frac_v[t, 0:1].astype(F32), field)
+        field = jnp.where(row == 3, frac_v[t, 1:2].astype(F32), field)
+        field = jnp.where(row == 4, var_v[...].astype(F32), field)
+        fields.append(jnp.where(row == 5, 1.0, field).astype(BF16))
     for k in range(DEPTH):
         z_to = lax.rem(z + distance_at(k), DEPTH)
-        pick = jnp.where((code == z_to * 8 + lane % 8) & mine, 1.0, 0.0).astype(BF16)
-        meta[k] = jnp.dot(fields[...], pick, preferred_element_type=F32)
+        total = jnp.zeros((8, PIX), F32)
+        for t in range(2):
+            chosen = (codes[t] == (z_to * 8).astype(F32) + place) & mine
+            pick = jnp.where(chosen, 1.0, 0.0).astype(BF16)
+            total = total + jnp.dot(fields[t], pick, preferred_element_type=F32)
+        meta[k] = total
+    move.wait()
 
 
 class Copies:
@@ -202,8 +195,8 @@
 
 
 def share_kernel(
-    tiles, meta, out,
-    core_in, relay1, fin1, blocks2, relay2, fin2, blocks3, far_in,
+    table, offs, shares, matched, meta, out,
+    core_out, core_in, relay1, fin1, blocks2, relay2, fin2, blocks3, far_in,
     meta_z, meta_x, meta_y, meta_c, send_sem, recv_sem,
 ):
     x, y, z, c = position()
@@ -214,34 +207,84 @@
     barrier = pltpu.get_barrier_semaphore()
     for peer in peers:
         pl.semaphore_signal(barrier, inc=1, device_id=peer, device_id_type=MESH)
-    pl.semaphore_wait(barrier, len(peers))
+
+    across_at = (iota((PIX, PPIX), 1) - iota((PIX, PPIX), 0)).astype(F32).astype(BF16)
+    down_at = (iota((PPIX, PIX), 0) - iota((PPIX, PIX), 1)).astype(F32).astype(BF16)
+
+    def one_hot(at, offset, share):
+        full = lambda value: jnp.full(at.shape, value, F32).astype(BF16)
+        offset = offset.astype(F32)
+        second = jnp.where(at == full(offset + 1.0), full(share), full(0.0))
+        return jnp.where(at == full(offset), full(1.0 - share), second)
+
+    def place(q, r):
+        slots = {}
+        for i in range(4):
+            for y_lo in range(2):
+                z_to = lax.rem(z + distance_at(4 * q + i), DEPTH)
+                p = z_to * 4 + y_lo * 2 + (c if r == 0 else 1 - c)
+                for slot in range(2):
+                    s = table[2 * p + slot]
+                    filled = s >= 0
+                    s = jnp.maximum(s, 0)
+                    t, b = s % 2, s // 2
+                    scale = jnp.where(filled, shares[4, b], 0.0)
+                    across = one_hot(across_at, offs[t, 1, b], shares[2 * t + 1, b])
+                    wide = jnp.dot(matched[b], across, preferred_element_type=F32)
+                    slots[i, y_lo, slot] = (s, (scale * wide).astype(BF16))
+        for i in range(4):
+            for y_lo in range(2):
+                downs = []
+                for slot in range(2):
+                    s = slots[i, y_lo, slot][0]
+                    t, b = s % 2, s // 2
+                    downs.append(one_hot(down_at, offs[t, 0, b], shares[2 * t, b]))
+                tile = jnp.dot(
+                    jnp.concatenate(downs, axis=1),
+                    jnp.concatenate([slots[i, y_lo, slot][1] for slot in range(2)], axis=0),
+                    preferred_element_type=F32,
+                )
+                for x_to in range(4):
+                    for y_hi in range(2):
+                        at = (x_to * 2 + y_hi) * ROWS
+                        y_to = y_hi * 2 + y_lo
+                        for half in range(2):
+                            block = tile[at : at + ROWS, half * PIX : (half + 1) * PIX]
+                            to = (x_to, i, y_to) if half == 0 else (y_to, i, x_to)
+                            if r == 1:
+                                core_out[(q, half) + to] = block.astype(BF16)
+                            else:
+                                block = block + core_in[(q, half) + to].astype(F32)
+                                core_in[(q, half) + to] = block.astype(BF16)
 
     copies = Copies(send_sem, recv_sem)
     x_device = lambda to: device_at(to, y, z, c)
     y_device = lambda to: device_at(x, to, z, c)
     z_device = lambda k: device_at(x, y, (z + distance_at(k)) % DEPTH, c)
 
-    core = [
-        copies.new(tiles.at[1, q], core_in.at[q], device_at(x, y, z, 1 - c)) for q in range(PARTS)
-    ]
-    for copy in core:
+    core, meta_copies = [], []
+
+    def send(q):
+        place(q, 1)
+        if q == 0:
+            pl.semaphore_wait(barrier, len(peers))
+        copy = copies.new(core_out.at[q], core_in.at[q], device_at(x, y, z, 1 - c))
         copy.start()
-
-    meta_copies = [copies.new(meta.at[k], meta_z.at[k], z_device(k)) for k in range(DEPTH - 1)]
-    for copy in meta_copies:
-        copy.start()
-    meta_z[DEPTH - 1] = meta[DEPTH - 1]
+        core.append(copy)
+
+    def meta_depth():
+        for k in range(DEPTH - 1):
+            copy = copies.new(meta.at[k], meta_z.at[k], z_device(k))
+            copy.start()
+            meta_copies.append(copy)
+        meta_z[DEPTH - 1] = meta[DEPTH - 1]
 
     rings1, rings2, sent3 = {}, {}, []
 
     def enter(q):
         core[q].wait_recv()
 
-        for half in range(2):
-            @pl.loop(0, 4)
-            def _(i, half=half):
-                add_into(core_in.at[q, half, i], tiles.at[0, q, half, i])
-
+        place(q, 0)
         for half in range(2):
             me, device = ((x, x_device), (y, y_device))[half]
             rings1[q, half] = Ring(
@@ -323,20 +366,25 @@
         meta_copies.append(copy)
         return copy
 
+    send(0)
+    send(1)
+    meta_depth()
     enter(0)
+    send(2)
+    middle(0)
     enter(1)
-    middle(0)
+    send(3)
     sent_x = meta_plane()
-    enter(2)
     turn(0)
     middle(1)
+    enter(2)
     sent_y = meta_second(sent_x)
-    enter(3)
     middle2(0)
     turn(1)
     middle(2)
+    enter(3)
+    leave(0)
     sent_c = meta_third(sent_y)
-    leave(0)
     middle2(1)
     turn(2)
     middle(3)
@@ -395,57 +443,36 @@
 
 
 def body(images, intersection, offsets, subpixel, variance, basis_index, coefficients):
-    target = intersection[0].reshape(PAIRS)
-    shifts = offsets[0].reshape(PAIRS, 2)
-    shares = subpixel[0].reshape(PAIRS, 2).astype(F32)
-    inverse = 1.0 / variance[0].astype(F32)
-    spare = jnp.zeros((PAIRS,), BF16)
-    fields = jnp.stack(
-        [
-            shifts[:, 0].astype(BF16),
-            shifts[:, 1].astype(BF16),
-            subpixel[0].reshape(PAIRS, 2)[:, 0],
-            subpixel[0].reshape(PAIRS, 2)[:, 1],
-            jnp.repeat(variance[0], 2),
-            spare + 1,
-            spare,
-            spare,
-        ]
-    )
+    inter = intersection[0].T
+    offs = jnp.transpose(offsets[0], (1, 2, 0))
+    frac = jnp.transpose(subpixel[0], (1, 2, 0))
+    coef = jnp.transpose(coefficients, (1, 2, 0))
     smem = pl.BlockSpec(memory_space=pltpu.SMEM)
     vmem = pl.BlockSpec(memory_space=pltpu.VMEM)
-    tiles, meta = pl.pallas_call(
-        local_kernel,
+    matched, table, shares, meta = pl.pallas_call(
+        match_kernel,
         out_shape=(
-            jax.ShapeDtypeStruct((2, PARTS, 2, 4, 4, 4, ROWS, PIX), BF16),
+            jax.ShapeDtypeStruct((CELLS, PIX, PIX), BF16),
+            jax.ShapeDtypeStruct((2 * PATCHES,), I32),
+            jax.ShapeDtypeStruct((8, PIX), F32),
             jax.ShapeDtypeStruct((DEPTH, 8, PIX), F32),
         ),
-        in_specs=[smem] * 6 + [vmem] * 4,
-        out_specs=(vmem, vmem),
+        in_specs=[smem] * 4 + [vmem] * 5,
+        out_specs=(vmem, smem, smem, vmem),
         scratch_shapes=[
-            pltpu.VMEM((CELLS, PIX, PIX), BF16),
-            pltpu.SMEM((2 * PATCHES,), I32),
+            pltpu.VMEM((8, PIX), F32),
             pltpu.SMEM((PATCHES,), I32),
+            pltpu.SemaphoreType.DMA,
         ],
         compiler_params=pltpu.CompilerParams(vmem_limit_bytes=VMEM_LIMIT),
-    )(
-        target,
-        shifts.reshape(2 * PAIRS),
-        shares.reshape(2 * PAIRS),
-        inverse,
-        basis_index[0],
-        coefficients.reshape(-1),
-        images[0],
-        target.reshape(1, PAIRS),
-        target.reshape(PAIRS, 1),
-        fields,
-    )
+    )(inter, offs, basis_index, coef, images[0], inter, offs, frac, variance)
     out = pl.pallas_call(
         share_kernel,
         out_shape=jax.ShapeDtypeStruct((ROWS, PPIX), F32),
-        in_specs=[vmem] * 2,
+        in_specs=[smem] * 3 + [vmem] * 2,
         out_specs=vmem,
         scratch_shapes=[
+            pltpu.VMEM((PARTS, 2, 4, 4, 4, ROWS, PIX), BF16),
             pltpu.VMEM((PARTS, 2, 4, 4, 4, ROWS, PIX), BF16),
             pltpu.VMEM((PARTS, 2, 2, 2, 4, ROWS, PIX), BF16),
             pltpu.VMEM((PARTS, 2, 2, 4, 4, ROWS, PIX), BF16),
@@ -464,7 +491,7 @@
         compiler_params=pltpu.CompilerParams(
             collective_id=0, has_side_effects=True, vmem_limit_bytes=VMEM_LIMIT
         ),
-    )(tiles, meta)
+    )(table, offs, shares, matched, meta)
     return out[None]
 
 

time: 98.9 us -> 66.9 us (0.68)
  the two profiles are of different devices: /device:TPU:1 before, /device:TPU:2 now
where the time goes in v2:
time: 66.9 us; the launch traced here: 66.7 us
  Pallas kernels  65.3 us (98%)
  local copies, waits for them, and re-layouts  1.38 us (2%)
    pallas_call x1, Pallas kernels, body(): pl.pallas_call(share_kernel, out_shape=jax.ShapeDtypeStruct((ROWS, PPIX),...  59.2 us
    pallas_call x1, Pallas kernels, body(): pl.pallas_call(match_kernel, out_shape=(jax.ShapeDtypeStruct((CELLS, PIX,...  6.09 us
    unnamed x1, local copies, waits for them, and re-layouts  1.38 us

profile of v2, /device:TPU:2, one launch (start us, length us, event | category | flops | bytes accessed | tf_op | source)
XLA Modules:
  0.0 66.7 jit_solution(7143980857571431792)
XLA Ops:
  0.0 6.1 %shard_map.73 = (bf16[32,128,128]{2,1,0:T(8,128)(2,1)}, s32[128]{0:T(128)}, f32[8,128]{1,0:T(8,128)}, f32[16,8,128]{2,1,0:T(8,128)}) custom-call(s32[2,32]{1,0:T(2,128)} %bitcast.18, s32[2,2,32]{2,1,0:T(2,128)} %bitcast.14, s32[1,32]{1,0:T(1,128)} %basis.1, f32[3,3,64]{2,1,0:T(4,128)} %bitcast.17, bf16[32,128,128]{2,1,0:T(8,128)(2,1)} %bitcast.12, ...), custom_call_target="tpu_custom_call" | custom-call | tf_op jit(solution)/shard_map/pallas_call | solution.py:452
  6.1 59.2 %shard_map.74 = f32[32,256]{1,0:T(8,128)} custom-call(s32[128]{0:T(128)} %get-tuple-element.9.table, s32[2,2,32]{2,1,0:T(2,128)} %bitcast.16, f32[8,128]{1,0:T(8,128)} %get-tuple-element.10.shares, bf16[32,128,128]{2,1,0:T(8,128)(2,1)} %get-tuple-element.11.matched, f32[16,8,128]{2,1,0:T(8,128)} %get-tuple-element.12.meta), custom_call_target="tpu_custom_call" | custom-call | tf_op jit(solution)/shard_map/pallas_call | solution.py:469
  65.3 1.4 %copy.9 = f32[1,32,256]{2,1,0:T(8,128)} copy(f32[1,32,256]{2,1,0:T(8,128)} %bitcast.13) | data formatting | bytes 65536

commit v3 on v2

v3 whole, which is shorter than its diff:
```python
import math

import jax
import jax.numpy as jnp
from jax import lax
from jax.experimental import pallas as pl
from jax.experimental.pallas import tpu as pltpu
from jax.sharding import PartitionSpec as P

PIX = 128
PPIX = 256
NB = 3
CELLS = 32
PATCHES = 64
DEPTH = 16
CHUNKS = (2, 4, 4, 4, 2)
ROWS = 32
F32, BF16, I32 = jnp.float32, jnp.bfloat16, jnp.int32
MESH = pl.DeviceIdType.MESH
GROUP = 8
VMEM_LIMIT = 56 * 1024 * 1024


def distance_at(k):
    if isinstance(k, int):
        return 8 + k // 2 if k % 2 == 0 else 7 - k // 2
    return jnp.where(k % 2 == 0, 8 + k // 2, 7 - k // 2)


def position():
    v, p = lax.axis_index("visit"), lax.axis_index("patch")
    return v // 2, (v % 2) * 2 + (p // 2) % 2, p // 4, p % 2


def device_at(x, y, z, c):
    return {"visit": x * 2 + y // 2, "patch": z * 4 + (y % 2) * 2 + c}


def iota(shape, axis):
    return lax.broadcasted_iota(I32, shape, axis)


class Copies:
    def __init__(self, send, recv):
        self.send, self.recv, self.used = send, recv, 0

    def new(self, src, dst, device):
        at = self.used
        self.used += 1
        return pltpu.make_async_remote_copy(
            src_ref=src,
            dst_ref=dst,
            send_sem=self.send.at[at],
            recv_sem=self.recv.at[at],
            device_id=device,
            device_id_type=MESH,
        )


def add_into(dst, src):
    dst[...] = (dst[...].astype(F32) + src[...].astype(F32)).astype(BF16)


class Ring:
    def __init__(self, copies, me, device, blocks, relay, fin):
        half = blocks.shape[1] // 2
        lo, hi = pl.ds(0, half), pl.ds(half, half)
        right, left, far = (me + 1) % 4, (me + 3) % 4, (me + 2) % 4
        to_right, to_left = device(right), device(left)
        self.blocks, self.relay, self.fin = blocks, relay, fin
        self.me, self.left, self.right, self.lo, self.hi = me, left, right, lo, hi
        self.first = [
            copies.new(blocks.at[far, lo], relay.at[0], to_right),
            copies.new(blocks.at[far, hi], relay.at[1], to_left),
            copies.new(blocks.at[right, hi], fin.at[0, hi], to_right),
            copies.new(blocks.at[left, lo], fin.at[1, lo], to_left),
        ]
        self.second = [
            copies.new(blocks.at[right, lo], fin.at[0, lo], to_right),
            copies.new(blocks.at[left, hi], fin.at[1, hi], to_left),
        ]

    def start(self):
        for copy in self.first:
            copy.start()

    def forward(self):
        self.first[0].wait_recv()
        add_into(self.blocks.at[self.right, self.lo], self.relay.at[0])
        self.second[0].start()
        self.first[1].wait_recv()
        add_into(self.blocks.at[self.left, self.hi], self.relay.at[1])
        self.second[1].start()

    def finish(self):
        for copy in self.first[2:] + self.second:
            copy.wait_recv()

    def result(self, i):
        own = self.blocks[self.me, i].astype(F32)
        return own + self.fin[0, i].astype(F32) + self.fin[1, i].astype(F32)

    def drain(self):
        for copy in self.first + self.second:
            copy.wait_send()


class Exchange:
    def __init__(self, copies, me, device, blocks, fin):
        self.me, self.blocks, self.fin = me, blocks, fin
        self.all = []
        for d in (2, 1, 3):
            to = (me + d) % 4
            self.all.append(copies.new(blocks.at[to], fin.at[d - 1], device(to)))

    def start(self):
        for copy in self.all:
            copy.start()

    def finish(self):
        for copy in self.all:
            copy.wait_recv()

    def result(self, i):
        total = self.blocks[self.me, i].astype(F32)
        for d in range(3):
            total = total + self.fin[d, i].astype(F32)
        return total

    def drain(self):
        for copy in self.all:
            copy.wait_send()


def coadd_kernel(
    basis, coef, images, inter, offs, frac, var, out,
    matched, slots_i, slots_f, table_i, table_f, meta, far_out, far_in,
    meta_z, meta_x, meta_y, meta_c, send_sem, recv_sem, move_sem, *chunk_refs,
):
    x, y, z, c = position()
    partner = device_at(x, y, z, 1 - c)
    x_device = lambda to: device_at(to, y, z, c)
    y_device = lambda to: device_at(x, to, z, c)
    z_device = lambda k: device_at(x, y, (z + distance_at(k)) % DEPTH, c)
    peers = [partner]
    peers += [x_device((x + d) % 4) for d in (1, 2, 3)]
    peers += [y_device((y + d) % 4) for d in (1, 2, 3)]
    peers += [z_device(k) for k in range(DEPTH - 1)]
    barrier = pltpu.get_barrier_semaphore()
    for peer in peers:
        pl.semaphore_signal(barrier, inc=1, device_id=peer, device_id_type=MESH)
    copies = Copies(send_sem, recv_sem)
    sent = []

    def start(copy):
        copy.start()
        sent.append(copy)
        return copy

    earlier = iota((CELLS, CELLS), 1) < iota((CELLS, CELLS), 0)
    diagonal = iota((CELLS, CELLS), 1) == iota((CELLS, CELLS), 0)
    lane = iota((CELLS, PIX), 1)
    cell = iota((CELLS, PIX), 0)
    row = iota((8, CELLS), 0)
    params = jnp.zeros((8, PIX), F32)
    cell_of = jnp.zeros((1, PIX), I32)
    for t in range(2):
        named = inter[t : t + 1]
        column = jnp.sum(jnp.where(diagonal, named, 0), axis=1, keepdims=True)
        code = 2 * column
        for other in range(2):
            same = (column == inter[other : other + 1]) & earlier
            code = code + jnp.sum(jnp.where(same, 1, 0), axis=1, keepdims=True)
        chosen = code == lane
        here = jnp.max(jnp.where(chosen, cell, 0), axis=0, keepdims=True)
        cell_of = jnp.maximum(cell_of, here)
        field = jnp.where(row == 0, offs[t, 0:1].astype(F32), 0.0)
        field = jnp.where(row == 1, offs[t, 1:2].astype(F32), field)
        field = jnp.where(row == 2, frac[t, 0:1].astype(F32), field)
        field = jnp.where(row == 3, frac[t, 1:2].astype(F32), field)
        field = jnp.where(row == 4, var[...].astype(F32), field)
        field = jnp.where(row == 5, 1.0, field).astype(BF16)
        pick = jnp.where(chosen, 1.0, 0.0).astype(BF16)
        params = params + jnp.dot(field, pick, preferred_element_type=F32)
    valid = params[5:6] > 0.0
    scale = jnp.where(valid, 1.0 / jnp.where(valid, params[4:5], 1.0), 0.0)
    slots_i[0] = jnp.broadcast_to(cell_of, (8, PIX))
    slots_f[0] = jnp.where(iota((8, PIX), 0) == 4, scale, params)
    own_moves = [
        pltpu.make_async_copy(slots_i.at[0], table_i.at[0], move_sem.at[0]),
        pltpu.make_async_copy(slots_f.at[0], table_f.at[0], move_sem.at[1]),
    ]
    for move in own_moves:
        move.start()
    my_lanes = iota((8, PIX), 1) // 8 == z
    for k in range(DEPTH):
        z_to = lax.rem(z + distance_at(k), DEPTH)
        turned = pltpu.roll(params, lax.rem(8 * (z - z_to) + PIX, PIX), 1)
        meta[k] = jnp.where(my_lanes, turned, 0.0)

    spread = (iota((PIX, PIX), 0) - iota((PIX, PIX), 1)).astype(F32)
    kernels = []
    for k in range(NB):
        width = 2.0**k
        profile = jnp.exp(-(spread**2) / (2.0 * width**2))
        kernels.append((profile / (math.sqrt(2.0 * math.pi) * width)).astype(BF16))
    stacked = jnp.concatenate(kernels, axis=1)
    ramp_i = (2.0 * iota((PIX, PIX), 0).astype(F32) - (PIX - 1)) / (PIX - 1)
    ramp_j = (2.0 * iota((PIX, PIX), 1).astype(F32) - (PIX - 1)) / (PIX - 1)

    def match(g):
        rows = jnp.dot(
            images[pl.ds(GROUP * g, GROUP)].reshape(GROUP * PIX, PIX),
            stacked,
            preferred_element_type=F32,
        ).astype(BF16)
        total = [None] * GROUP
        for k in range(NB):
            part = rows[:, k * PIX : (k + 1) * PIX]
            wide = jnp.concatenate([part[b * PIX : (b + 1) * PIX] for b in range(GROUP)], axis=1)
            smooth = jnp.dot(kernels[k], wide, preferred_element_type=F32)
            for b in range(GROUP):
                q = basis[0, GROUP * g + b]
                mix = coef[k, 0, q] + coef[k, 1, q] * ramp_i + coef[k, 2, q] * ramp_j
                term = mix * smooth[:, b * PIX : (b + 1) * PIX]
                total[b] = term if k == 0 else total[b] + term
        for b in range(GROUP):
            matched[0, GROUP * g + b] = total[b].astype(BF16)

    cells_in = []

    def send_cells(group):
        cells_in.append(start(copies.new(matched.at[0, group], matched.at[1, group], partner)))

    @pl.loop(0, 2)
    def _(g):
        match(g)

    pl.semaphore_wait(barrier, len(peers))
    send_cells(pl.ds(0, 2 * GROUP))
    tables_in = [
        start(copies.new(slots_i.at[0], slots_i.at[1], partner)),
        start(copies.new(slots_f.at[0], slots_f.at[1], partner)),
    ]
    depth_in = [start(copies.new(meta.at[k], meta_z.at[k], z_device(k))) for k in range(DEPTH - 1)]
    meta_z[DEPTH - 1] = meta[DEPTH - 1]
    for g in (2, 3):
        match(g)
        send_cells(pl.ds(g * GROUP, GROUP))

    for move in own_moves:
        move.wait()
    for copy in tables_in:
        copy.wait_recv()
    other_moves = [
        pltpu.make_async_copy(slots_i.at[1], table_i.at[1], move_sem.at[2]),
        pltpu.make_async_copy(slots_f.at[1], table_f.at[1], move_sem.at[3]),
    ]
    for move in other_moves:
        move.start()
    for move in other_moves:
        move.wait()
    for copy in cells_in:
        copy.wait_recv()

    across_at = (iota((PIX, PPIX), 1) - iota((PIX, PPIX), 0)).astype(F32).astype(BF16)
    down_at = (iota((PPIX, PIX), 0) - iota((PPIX, PIX), 1)).astype(F32).astype(BF16)

    def one_hot(at, offset, share):
        full = lambda value: jnp.full(at.shape, value, F32).astype(BF16)
        second = jnp.where(at == full(offset + 1.0), full(share), full(0.0))
        return jnp.where(at == full(offset), full(1.0 - share), second)

    count = len(CHUNKS)
    first = [sum(CHUNKS[:q]) for q in range(count)]
    refs = [chunk_refs[5 * q : 5 * q + 5] for q in range(count)]
    rings1, rings2, last = {}, {}, []

    def place(q, blocks):
        pieces = {}
        for i in range(CHUNKS[q]):
            z_to = lax.rem(z + distance_at(first[q] + i), DEPTH)
            for y_lo in range(2):
                slot = 2 * (z_to * 4 + y_lo * 2 + c)
                for source in range(2):
                    for r in range(2):
                        field = lambda f: table_f[source, f, slot + r]
                        across = one_hot(across_at, field(1), field(3))
                        wide = jnp.dot(
                            matched[source, table_i[source, 0, slot + r]],
                            across,
                            preferred_element_type=F32,
                        )
                        pieces[i, y_lo, source, r] = (field(4) * wide).astype(BF16)
        for i in range(CHUNKS[q]):
            z_to = lax.rem(z + distance_at(first[q] + i), DEPTH)
            for y_lo in range(2):
                slot = 2 * (z_to * 4 + y_lo * 2 + c)
                downs, placed = [], []
                for source in range(2):
                    for r in range(2):
                        field = lambda f: table_f[source, f, slot + r]
                        downs.append(one_hot(down_at, field(0), field(2)))
                        placed.append(pieces[i, y_lo, source, r])
                tile = jnp.dot(
                    jnp.concatenate(downs, axis=1),
                    jnp.concatenate(placed, axis=0),
                    preferred_element_type=F32,
                ).astype(BF16)
                for x_to in range(4):
                    for y_hi in range(2):
                        at = (x_to * 2 + y_hi) * ROWS
                        y_to = y_hi * 2 + y_lo
                        blocks[0, x_to, i, y_to] = tile[at : at + ROWS, :PIX]
                        blocks[1, y_to, i, x_to] = tile[at : at + ROWS, PIX:]

    def enter(q):
        blocks, relay, fin = refs[q][:3]
        place(q, blocks)
        for half in range(2):
            me, device = ((x, x_device), (y, y_device))[half]
            ring = Ring(copies, me, device, blocks.at[half], relay.at[half], fin.at[half])
            ring.start()
            rings1[q, half] = ring

    def forward(q):
        for half in range(2):
            rings1[q, half].forward()

    def turn(q):
        blocks, fin = refs[q][3:5]
        for half in range(2):
            ring = rings1[q, half]
            ring.finish()
            for i in range(CHUNKS[q]):
                block = ring.result(i).astype(BF16)
                for other in range(4):
                    blocks[half, other, i] = block[other]
            me, device = ((y, y_device), (x, x_device))[half]
            rings2[q, half] = Exchange(copies, me, device, blocks.at[half], fin.at[half])
            rings2[q, half].start()

    def leave(q):
        for half in range(2):
            ring = rings2[q, half]
            ring.finish()
            for i in range(CHUNKS[q]):
                k = first[q] + i
                to = far_out if k < DEPTH - 1 else far_in
                to[k, half] = ring.result(i).astype(BF16)
        for i in range(CHUNKS[q]):
            k = first[q] + i
            if k < DEPTH - 1:
                last.append(start(copies.new(far_out.at[k], far_in.at[k], z_device(k))))

    def meta_first():
        for copy in depth_in:
            copy.wait_recv()
        total = meta_z[0]
        for k in range(1, DEPTH):
            total = total + meta_z[k]
        meta_x[x] = total
        return [
            start(copies.new(meta_x.at[x], meta_x.at[x], x_device((x + d) % 4))) for d in (1, 2, 3)
        ]

    def meta_second(before):
        for copy in before:
            copy.wait_recv()
        meta_y[y] = meta_x[...]
        return [
            start(copies.new(meta_y.at[y], meta_y.at[y], y_device((y + d) % 4))) for d in (1, 2, 3)
        ]

    def meta_third(before):
        for copy in before:
            copy.wait_recv()
        return start(copies.new(meta_y, meta_c, partner))

    enter(0)
    enter(1)
    forward(0)
    enter(2)
    sent_x = meta_first()
    forward(1)
    turn(0)
    enter(3)
    sent_y = meta_second(sent_x)
    forward(2)
    turn(1)
    leave(0)
    enter(4)
    sent_c = meta_third(sent_y)
    forward(3)
    turn(2)
    leave(1)
    forward(4)
    turn(3)
    leave(2)

    sent_c.wait_recv()
    combo = (y % 2) * 2 + c
    mine = (iota((8, PIX), 1) // 2) % 4 == combo
    row_at = (iota((ROWS, PIX), 0) + (x * 2 + y // 2) * ROWS).astype(F32)
    column_at = iota((PPIX, PIX), 0).astype(F32)

    def cover(at, offset, share):
        rest = (1.0 - share).astype(BF16).astype(F32)
        d = at - offset
        once = jnp.where((d >= 0.0) & (d < float(PIX)), rest, 0.0)
        return once + jnp.where((d >= 1.0) & (d < float(PIX + 1)), share, 0.0)

    weight = jnp.zeros((ROWS, PPIX), F32)
    for source in (meta_y, meta_c):
        for b in range(4):
            full = jnp.zeros((8, PIX), F32)
            for m in range(4):
                kept = jnp.where(mine, source[b, m], 0.0)
                full = full + pltpu.roll(kept, lax.rem(2 * (m - combo) + PIX, PIX), 1)
            there = full[5:6] > 0.0
            inverse = jnp.where(there, 1.0 / jnp.where(there, full[4:5], 1.0), 0.0)
            down = inverse * cover(row_at, full[0:1], full[2:3])
            across = cover(column_at, full[1:2], full[3:4])
            weight = weight + lax.dot_general(
                down, across, (((1,), (1,)), ((), ())),
                precision=lax.Precision.HIGHEST, preferred_element_type=F32,
            )

    turn(4)
    leave(3)
    leave(4)
    for copy in last:
        copy.wait_recv()
    for half in range(2):
        total = far_in[0, half].astype(F32)
        for k in range(1, DEPTH):
            total = total + far_in[k, half].astype(F32)
        columns = slice(half * PIX, (half + 1) * PIX)
        out[:, columns] = total / jnp.sqrt(weight[:, columns] + 1.0)

    for copy in sent:
        copy.wait_send()
    for ring in list(rings1.values()) + list(rings2.values()):
        ring.drain()


COPY_COUNT = 3 + 2 + (DEPTH - 1) * 2 + 7 + len(CHUNKS) * 18


def chunk_shapes(n):
    return [
        pltpu.VMEM((2, 4, n, 4, ROWS, PIX), BF16),
        pltpu.VMEM((2, 2, n // 2, 4, ROWS, PIX), BF16),
        pltpu.VMEM((2, 2, n, 4, ROWS, PIX), BF16),
        pltpu.VMEM((2, 4, n, ROWS, PIX), BF16),
        pltpu.VMEM((2, 3, n, ROWS, PIX), BF16),
    ]


def body(images, intersection, offsets, subpixel, variance, basis_index, coefficients):
    smem = pl.BlockSpec(memory_space=pltpu.SMEM)
    vmem = pl.BlockSpec(memory_space=pltpu.VMEM)
    scratch = [
        pltpu.VMEM((2, CELLS, PIX, PIX), BF16),
        pltpu.VMEM((2, 8, PIX), I32),
        pltpu.VMEM((2, 8, PIX), F32),
        pltpu.SMEM((2, 8, PIX), I32),
        pltpu.SMEM((2, 8, PIX), F32),
        pltpu.VMEM((DEPTH, 8, PIX), F32),
        pltpu.VMEM((DEPTH - 1, 2, ROWS, PIX), BF16),
        pltpu.VMEM((DEPTH, 2, ROWS, PIX), BF16),
        pltpu.VMEM((DEPTH, 8, PIX), F32),
        pltpu.VMEM((4, 8, PIX), F32),
        pltpu.VMEM((4, 4, 8, PIX), F32),
        pltpu.VMEM((4, 4, 8, PIX), F32),
        pltpu.SemaphoreType.DMA((COPY_COUNT,)),
        pltpu.SemaphoreType.DMA((COPY_COUNT,)),
        pltpu.SemaphoreType.DMA((4,)),
    ]
    for n in CHUNKS:
        scratch += chunk_shapes(n)
    out = pl.pallas_call(
        coadd_kernel,
        out_shape=jax.ShapeDtypeStruct((ROWS, PPIX), F32),
        in_specs=[smem] * 2 + [vmem] * 5,
        out_specs=vmem,
        scratch_shapes=scratch,
        compiler_params=pltpu.CompilerParams(
            collective_id=0, has_side_effects=True, vmem_limit_bytes=VMEM_LIMIT
        ),
    )(
        basis_index,
        jnp.transpose(coefficients, (1, 2, 0)),
        images[0],
        intersection[0].T,
        jnp.transpose(offsets[0], (1, 2, 0)),
        jnp.transpose(subpixel[0], (1, 2, 0)),
        variance,
    )
    return out[None]


def solution(mesh):
    return jax.shard_map(
        body,
        mesh=mesh,
        in_specs=(
            P("visit", "patch", None, None),
            P("visit", "patch", None),
            P("visit", "patch", None, None),
            P("visit", "patch", None, None),
            P("visit", "patch"),
            P("visit", "patch"),
            P(),
        ),
        out_specs=P("patch", "visit", None),
        check_vma=False,
    )
```

time: 66.9 us -> 58.8 us (0.88)
  the two profiles are of different devices: /device:TPU:2 before, /device:TPU:1 now
where the time goes in v3:
time: 58.8 us; the launch traced here: 58.6 us
  Pallas kernels  57.2 us (97%)
  local copies, waits for them, and re-layouts  1.38 us (2%)
    pallas_call x1, Pallas kernels, body(): pl.pallas_call(coadd_kernel, out_shape=jax.ShapeDtypeStruct((ROWS, PPIX),...  57.2 us
    unnamed x1, local copies, waits for them, and re-layouts  1.38 us

profile of v3, /device:TPU:1, one launch (start us, length us, event | category | flops | bytes accessed | tf_op | source)
XLA Modules:
  0.0 58.6 jit_solution(421980763141951027)
XLA Ops:
  0.0 57.2 %shard_map.73 = f32[32,256]{1,0:T(8,128)} custom-call(s32[1,32]{1,0:T(1,128)} %basis.1, f32[3,3,64]{2,1,0:T(4,128)} %bitcast.14, bf16[32,128,128]{2,1,0:T(8,128)(2,1)} %bitcast.12, s32[2,32]{1,0:T(2,128)} %bitcast.16, s32[2,2,32]{2,1,0:T(2,128)} %bitcast.15, bf16[2,2,32]{2,1,0:T(2,128)(2,1)} %bitcast.17, bf16[1,32]{1,0:T(2,128)(2,1)} %var.1), custom_call_target="tpu_custom_call" | custom-call | tf_op jit(solution)/shard_map/pallas_call | solution.py:482
  57.2 1.4 %copy.9 = f32[1,32,256]{2,1,0:T(8,128)} copy(f32[1,32,256]{2,1,0:T(8,128)} %bitcast.13) | data formatting | bytes 65536

commit v4 on v3

--- a/solution.py
+++ b/solution.py
@@ -134,7 +134,7 @@
 
 def coadd_kernel(
     basis, coef, images, inter, offs, frac, var, out,
-    matched, slots_i, slots_f, table_i, table_f, meta, far_out, far_in,
+    pixels, matched, slots_i, slots_f, table_i, table_f, meta, far_out, far_in,
     meta_z, meta_x, meta_y, meta_c, send_sem, recv_sem, move_sem, *chunk_refs,
 ):
     x, y, z, c = position()
@@ -142,15 +142,22 @@
     x_device = lambda to: device_at(to, y, z, c)
     y_device = lambda to: device_at(x, to, z, c)
     z_device = lambda k: device_at(x, y, (z + distance_at(k)) % DEPTH, c)
-    peers = [partner]
-    peers += [x_device((x + d) % 4) for d in (1, 2, 3)]
-    peers += [y_device((y + d) % 4) for d in (1, 2, 3)]
-    peers += [z_device(k) for k in range(DEPTH - 1)]
+    peers = [z_device(k) for k in range(DEPTH - 1)]
+    peers += [x_device((x + d) % 4) for d in (2, 1, 3)]
+    peers += [y_device((y + d) % 4) for d in (2, 1, 3)]
+    peers += [partner]
     barrier = pltpu.get_barrier_semaphore()
     for peer in peers:
         pl.semaphore_signal(barrier, inc=1, device_id=peer, device_id_type=MESH)
     copies = Copies(send_sem, recv_sem)
     sent = []
+
+    def pixels_in(g):
+        cells = pl.ds(g * GROUP, GROUP)
+        return pltpu.make_async_copy(images.at[cells], pixels.at[cells], move_sem.at[4 + g])
+
+    for g in range(CELLS // GROUP):
+        pixels_in(g).start()
 
     def start(copy):
         copy.start()
@@ -209,8 +216,9 @@
     ramp_j = (2.0 * iota((PIX, PIX), 1).astype(F32) - (PIX - 1)) / (PIX - 1)
 
     def match(g):
+        pixels_in(g).wait()
         rows = jnp.dot(
-            images[pl.ds(GROUP * g, GROUP)].reshape(GROUP * PIX, PIX),
+            pixels[pl.ds(GROUP * g, GROUP)].reshape(GROUP * PIX, PIX),
             stacked,
             preferred_element_type=F32,
         ).astype(BF16)
@@ -461,6 +469,7 @@
     smem = pl.BlockSpec(memory_space=pltpu.SMEM)
     vmem = pl.BlockSpec(memory_space=pltpu.VMEM)
     scratch = [
+        pltpu.VMEM((CELLS, PIX, PIX), BF16),
         pltpu.VMEM((2, CELLS, PIX, PIX), BF16),
         pltpu.VMEM((2, 8, PIX), I32),
         pltpu.VMEM((2, 8, PIX), F32),
@@ -475,14 +484,14 @@
         pltpu.VMEM((4, 4, 8, PIX), F32),
         pltpu.SemaphoreType.DMA((COPY_COUNT,)),
         pltpu.SemaphoreType.DMA((COPY_COUNT,)),
-        pltpu.SemaphoreType.DMA((4,)),
+        pltpu.SemaphoreType.DMA((4 + CELLS // GROUP,)),
     ]
     for n in CHUNKS:
         scratch += chunk_shapes(n)
     out = pl.pallas_call(
         coadd_kernel,
         out_shape=jax.ShapeDtypeStruct((ROWS, PPIX), F32),
-        in_specs=[smem] * 2 + [vmem] * 5,
+        in_specs=[smem] * 2 + [pl.BlockSpec(memory_space=pl.ANY)] + [vmem] * 4,
         out_specs=vmem,
         scratch_shapes=scratch,
         compiler_params=pltpu.CompilerParams(

time: 58.8 us -> 58.7 us (level)
  no operation moved by 1% of the time
where the time goes in v4:
time: 58.7 us; the launch traced here: 58.5 us
  Pallas kernels  57.1 us (97%)
  local copies, waits for them, and re-layouts  1.38 us (2%)
    pallas_call x1, Pallas kernels, body(): pl.pallas_call(coadd_kernel, out_shape=jax.ShapeDtypeStruct((ROWS, PPIX),...  57.1 us
    unnamed x1, local copies, waits for them, and re-layouts  1.38 us

profile of v4, /device:TPU:1, one launch (start us, length us, event | category | flops | bytes accessed | tf_op | source)
XLA Modules:
  0.0 58.5 jit_solution(15943398274940399096)
XLA Ops:
  0.0 57.1 %shard_map.73 = f32[32,256]{1,0:T(8,128)} custom-call(s32[1,32]{1,0:T(1,128)} %basis.1, f32[3,3,64]{2,1,0:T(4,128)} %bitcast.14, bf16[32,128,128]{2,1,0:T(8,128)(2,1)} %bitcast.12, s32[2,32]{1,0:T(2,128)} %bitcast.16, s32[2,2,32]{2,1,0:T(2,128)} %bitcast.15, bf16[2,2,32]{2,1,0:T(2,128)(2,1)} %bitcast.17, bf16[1,32]{1,0:T(2,128)(2,1)} %var.1), custom_call_target="tpu_custom_call" | custom-call | tf_op jit(solution)/shard_map/pallas_call | solution.py:491
  57.1 1.4 %copy.9 = f32[1,32,256]{2,1,0:T(8,128)} copy(f32[1,32,256]{2,1,0:T(8,128)} %bitcast.13) | data formatting | bytes 65536

commit v5 on v3

--- a/solution.py
+++ b/solution.py
@@ -14,6 +14,7 @@
 PATCHES = 64
 DEPTH = 16
 CHUNKS = (2, 4, 4, 4, 2)
+RING_PARTS = 3
 ROWS = 32
 F32, BF16, I32 = jnp.float32, jnp.bfloat16, jnp.int32
 MESH = pl.DeviceIdType.MESH
@@ -273,7 +274,7 @@
 
     count = len(CHUNKS)
     first = [sum(CHUNKS[:q]) for q in range(count)]
-    refs = [chunk_refs[5 * q : 5 * q + 5] for q in range(count)]
+    refs = [chunk_refs[6 * q : 6 * q + 6] for q in range(count)]
     rings1, rings2, last = {}, {}, []
 
     def place(q, blocks):
@@ -328,7 +329,7 @@
             rings1[q, half].forward()
 
     def turn(q):
-        blocks, fin = refs[q][3:5]
+        blocks, fin, relay = refs[q][3:6]
         for half in range(2):
             ring = rings1[q, half]
             ring.finish()
@@ -337,8 +338,16 @@
                 for other in range(4):
                     blocks[half, other, i] = block[other]
             me, device = ((y, y_device), (x, x_device))[half]
-            rings2[q, half] = Exchange(copies, me, device, blocks.at[half], fin.at[half])
+            if q < RING_PARTS:
+                ring = Ring(copies, me, device, blocks.at[half], relay.at[half], fin.at[half])
+            else:
+                ring = Exchange(copies, me, device, blocks.at[half], fin.at[half])
+            rings2[q, half] = ring
             rings2[q, half].start()
+
+    def forward_second(q):
+        for half in range(2):
+            rings2[q, half].forward()
 
     def leave(q):
         for half in range(2):
@@ -387,14 +396,17 @@
     enter(3)
     sent_y = meta_second(sent_x)
     forward(2)
+    forward_second(0)
     turn(1)
+    enter(4)
     leave(0)
-    enter(4)
     sent_c = meta_third(sent_y)
     forward(3)
+    forward_second(1)
     turn(2)
     leave(1)
     forward(4)
+    forward_second(2)
     turn(3)
     leave(2)
 
@@ -444,7 +456,7 @@
         ring.drain()
 
 
-COPY_COUNT = 3 + 2 + (DEPTH - 1) * 2 + 7 + len(CHUNKS) * 18
+COPY_COUNT = 3 + 2 + (DEPTH - 1) * 2 + 7 + len(CHUNKS) * 24
 
 
 def chunk_shapes(n):
@@ -454,6 +466,7 @@
         pltpu.VMEM((2, 2, n, 4, ROWS, PIX), BF16),
         pltpu.VMEM((2, 4, n, ROWS, PIX), BF16),
         pltpu.VMEM((2, 3, n, ROWS, PIX), BF16),
+        pltpu.VMEM((2, 2, n // 2, ROWS, PIX), BF16),
     ]
 
 

time: 58.8 us -> 61.9 us (1.053)
  Pallas kernels: 57.2 us -> 60.3 us
    pallas_call x1, Pallas kernels: 57.2 us -> 60.3 us  [body(): pl.pallas_call(coadd_kernel, out_shape=jax.ShapeDtypeStruct((ROWS, PPIX),...]
where the time goes in v5:
time: 61.9 us; the launch traced here: 61.7 us
  Pallas kernels  60.3 us (97%)
  local copies, waits for them, and re-layouts  1.38 us (2%)
    pallas_call x1, Pallas kernels, body(): pl.pallas_call(coadd_kernel, out_shape=jax.ShapeDtypeStruct((ROWS, PPIX),...  60.3 us
    unnamed x1, local copies, waits for them, and re-layouts  1.38 us

profile of v5, /device:TPU:1, one launch (start us, length us, event | category | flops | bytes accessed | tf_op | source)
XLA Modules:
  0.0 61.7 jit_solution(6577193863825386273)
XLA Ops:
  0.0 60.3 %shard_map.73 = f32[32,256]{1,0:T(8,128)} custom-call(s32[1,32]{1,0:T(1,128)} %basis.1, f32[3,3,64]{2,1,0:T(4,128)} %bitcast.14, bf16[32,128,128]{2,1,0:T(8,128)(2,1)} %bitcast.12, s32[2,32]{1,0:T(2,128)} %bitcast.16, s32[2,2,32]{2,1,0:T(2,128)} %bitcast.15, bf16[2,2,32]{2,1,0:T(2,128)(2,1)} %bitcast.17, bf16[1,32]{1,0:T(2,128)(2,1)} %var.1), custom_call_target="tpu_custom_call" | custom-call | tf_op jit(solution)/shard_map/pallas_call | solution.py:495
  60.3 1.4 %copy.9 = f32[1,32,256]{2,1,0:T(8,128)} copy(f32[1,32,256]{2,1,0:T(8,128)} %bitcast.13) | data formatting | bytes 65536
